TPU v7x, 32 devices: a whole 2x2x4 slice. The times are simulated.
32 devices in a mesh: batch: 8 (over y, x, core), mp: 4 (over z).
Axes of the slice: x: 2, y: 2, z: 4, core: 2. Of those that a mesh axis runs over, the one named last changes fastest.
Arguments:
- residual: bfloat16 [8, 64, 8192], P('batch', None, 'mp'), may hold values from -6 to 6
- query_states: bfloat16 [8, 64, 4096], P('batch', None, 'mp')
- key_states: bfloat16 [8, 64, 512], P('batch')
- value_states: bfloat16 [8, 64, 512], P('batch'), may hold values from -6 to 6
- prompt_perm: int32 [8], replicated, may hold values from 0 to 7, each once
- ablated_heads: int32 [8], replicated, may hold values from 0 to 31, as said below
- out_weight: bfloat16 [4096, 8192], P('batch', 'mp'), may hold values from -0.09375 to 0.09375
- rms_gain: float32 [8192], P('mp'), may hold values from 0.1 to 1.9
- gate_weight: bfloat16 [8192, 14336], P('mp', 'batch'), may hold values from -0.0625 to 0.0625
- up_weight: bfloat16 [8192, 14336], P('mp', 'batch'), may hold values from -0.0625 to 0.0625
- down_weight: bfloat16 [14336, 8192], P('batch', 'mp'), may hold values from -0.046875 to 0.046875
Outputs:
- attn_out: bfloat16 [8, 64, 8192], P('batch', None, 'mp')
- mlp_out: bfloat16 [8, 64, 8192], P('batch', None, 'mp')
Inputs may be any that keep to these rules, and one draw needn't show every extreme that they name: `prompt_perm`: each prompt index appears exactly once. `ablated_heads`: 8 different head indices in any order, one of them 32 - 1.
All inputs are finite; a program needn't handle non-finite values.
Results may differ from a plain program's by a relative error of at most 0.035.
Values may be sent and summed in bfloat16 or wider, within the bound.
A program may use at most 128 MiB of HBM per device.

v0:
```python
import math
import jax
import jax.numpy as jnp
from jax import lax
from jax.sharding import PartitionSpec as P

D = 8192
HEADS = 32
KV = 4
HD = 128
ABLATED = 8


def local_heads(query_states, key_states, value_states):
    prompts_here, length, columns = query_states.shape
    head_count = columns // HD
    first_head = lax.axis_index("mp") * head_count
    owners = (first_head + jnp.arange(head_count)) // (HEADS // KV)
    query_four = query_states.reshape(prompts_here, length, head_count, HD)
    key_four = jnp.take(key_states.reshape(prompts_here, length, KV, HD), owners, axis=2)
    value_four = jnp.take(value_states.reshape(prompts_here, length, KV, HD), owners, axis=2)
    scores = jnp.einsum(
        "pshd,pthd->phst", query_four, key_four, preferred_element_type=jnp.float32
    ) / math.sqrt(HD)
    positions = jnp.arange(length)
    causal = positions[:, None] >= positions[None, :]
    scores = jnp.where(causal, scores, -1e30)
    highest = jnp.max(scores, axis=-1, keepdims=True)
    weights = jnp.exp(scores - highest)
    probability = (weights / jnp.sum(weights, axis=-1, keepdims=True)).astype(jnp.bfloat16)
    mixed_heads = jnp.einsum(
        "phst,pthd->pshd", probability, value_four, preferred_element_type=jnp.float32
    )
    return mixed_heads.astype(jnp.bfloat16).reshape(prompts_here, length, head_count * HD)


def body(
    residual,
    query_states,
    key_states,
    value_states,
    prompt_perm,
    ablated_heads,
    out_weight,
    rms_gain,
    gate_weight,
    up_weight,
    down_weight,
):
    prompts_here, length, model_cols = residual.shape
    local_rows = prompts_here * length
    head_block = local_heads(query_states, key_states, value_states)
    all_heads = lax.all_gather(head_block, "mp", axis=2, tiled=True)
    batch_index = lax.axis_index("batch")
    sources = jnp.take(prompt_perm, batch_index * prompts_here + jnp.arange(prompts_here))
    stacked = all_heads.reshape(prompts_here, length, HEADS, HD)
    picked_cols = jnp.take(stacked, ablated_heads, axis=2).reshape(
        prompts_here, length * ABLATED * HD
    )
    block_rows = lax.all_gather(picked_cols, "batch", axis=0, tiled=True)
    selector = (sources[:, None] == jnp.arange(block_rows.shape[0])[None, :]).astype(jnp.bfloat16)
    picked = jnp.dot(selector, block_rows, preferred_element_type=jnp.float32)
    picked_four = picked.astype(jnp.bfloat16).reshape(prompts_here, length, ABLATED, HD)
    placing = (jnp.arange(HEADS)[:, None] == ablated_heads[None, :]).astype(jnp.bfloat16)
    placed = jnp.einsum(
        "psad,ga->psgd", picked_four, placing, preferred_element_type=jnp.float32
    ).astype(jnp.bfloat16)
    chosen = jnp.any(jnp.arange(HEADS)[:, None] == ablated_heads[None, :], axis=1)
    mixed_heads = jnp.where(chosen[None, None, :, None], placed, stacked).reshape(
        local_rows, HEADS * HD
    )
    attn_float = jnp.dot(
        mixed_heads,
        lax.all_gather(out_weight, "batch", axis=0, tiled=True),
        preferred_element_type=jnp.float32,
    )
    attn_out = attn_float.astype(jnp.bfloat16)
    hidden_state = residual.reshape(local_rows, model_cols).astype(jnp.float32) + attn_float
    squares = lax.psum(jnp.sum(hidden_state * hidden_state, axis=1), "mp")
    inverse = lax.rsqrt(squares / D + 1e-05)
    normed = (hidden_state * inverse[:, None] * rms_gain[None, :]).astype(jnp.bfloat16)
    block_rows = lax.all_gather(normed, "batch", axis=0, tiled=True)
    gate_part = jnp.dot(block_rows, gate_weight, preferred_element_type=jnp.float32)
    up_part = jnp.dot(block_rows, up_weight, preferred_element_type=jnp.float32)
    partial_value = jnp.concatenate([gate_part, up_part], axis=1)
    slice_width = gate_weight.shape[1]
    summed = lax.psum(partial_value.astype(jnp.bfloat16), "mp").astype(jnp.float32)
    hidden = (jax.nn.silu(summed[:, :slice_width]) * summed[:, slice_width:]).astype(jnp.bfloat16)
    block_rows = hidden
    mlp_float = lax.psum_scatter(
        jnp.dot(block_rows, down_weight, preferred_element_type=jnp.float32).astype(jnp.bfloat16),
        "batch",
        scatter_dimension=0,
        tiled=True,
    )
    return (
        attn_out.reshape(prompts_here, length, model_cols),
        mlp_float.reshape(prompts_here, length, model_cols),
    )


def solution(mesh):
    placed = (
        P("batch", None, "mp"),
        P("batch", None, "mp"),
        P("batch", None, None),
        P("batch", None, None),
        P(),
        P(),
        P("batch", "mp"),
        P("mp"),
        P("mp", "batch"),
        P("mp", "batch"),
        P("batch", "mp"),
    )
    return jax.shard_map(
        body,
        mesh=mesh,
        in_specs=placed,
        out_specs=(P("batch", None, "mp"), P("batch", None, "mp")),
        check_vma=False,
    )
```

profile of v0, /device:TPU:0, one launch (start us, length us, event | category | flops | bytes accessed | tf_op | source)
XLA Modules:
  0.0 413.6 jit_solution(484651136919230348)
XLA Ops:
  7.2 0.0 copy-start
  7.2 0.0 all-gather.9.cloned.1.call-start
  7.3 0.7 compare_select_fusion.1
  7.9 0.7 compare_and_fusion.1
  8.6 0.9 copy.37
  9.6 0.6 gather_fusion.2
  10.2 0.3 fusion.7
  10.4 0.1 fusion.41
  10.5 0.9 bitcast_bitcast_fusion.1
  11.4 0.6 gather_fusion.1
  11.9 0.0 copy-start.6
  12.0 0.0 copy-start.4
  12.0 0.3 fusion.9
  12.3 17.4 %all_gather.12 = bf16[1,64,4096]{2,1,0:T(8,128)(2,1)S(1)} all-gather(bf16[1,64,1024]{2,1,0:T(8,128)(2,1)S(1)} %bitcast.109), channel_id=1, replica_groups=mesh['batch'=8,'mp'=4] {'mp'}, dimensions={2}, use_global_device_ids=true | all-gather | bytes 655360 | tf_op jit(solution)/shard_map/all_gather | solution.py:53
  29.6 0.1 copy.38
  29.7 0.0 copy-start.2
  29.7 0.2 copy.30
  30.0 0.6 gather_fusion
  30.5 0.1 select_bitcast_fusion
  30.6 0.1 copy.31
  30.7 0.8 reshape.200
  31.5 0.0 all-gather.9.cloned.1.call-update
  31.5 0.0 all-gather.5.cloned.1.call-start
  31.6 0.7 all-gather.5.cloned.1.call-update
  32.3 0.0 all-gather.7.cloned.1.call-start
  32.3 0.6 dynamic-slice.2
  33.5 0.1 fusion.30
  33.6 27.7 %all-gather.9.cloned.1.call-done = bf16[8,1,65536]{2,1,0:T(2,128)(2,1)} async-done(((bf16[1,1,65536]{2,1,0:T(2,128)(2,1)}), bf16[8,1,65536]{2,1,0:T(2,128)(2,1)}) %all-gather.9.cloned.1.call-update) | async-done | bytes 1048592 | tf_op jit(solution)/shard_map/all_gather | solution.py:60
  61.3 2.9 fusion.11
  64.2 0.4 fusion.10
  64.6 88.5 %all-gather.5.cloned.1.call-done = bf16[4096,2048]{1,0:T(8,128)(2,1)} async-done(((bf16[512,2048]{1,0:T(8,128)(2,1)}), bf16[4096,2048]{1,0:T(8,128)(2,1)}) %all-gather.5.cloned.1.call-update) | async-done | bytes 16777232 | tf_op jit(solution)/shard_map/all_gather | solution.py:74
  153.1 8.9 %multiply_reduce_fusion = (f32[64]{0:T(128)S(1)}, f32[64,2048]{1,0:T(8,128)S(1)}) fusion(bf16[1,64,2048]{2,1,0:T(8,128)(2,1)S(1)} %copy-done.2, bf16[4096,2048]{1,0:T(8,128)(2,1)} %all-gather.5.cloned.1.call-done, bf16[8,8,32,128]{3,2,1,0:T(8,128)(2,1)S(1)} %bitcast.106), kind=kOutput, calls=%fused_computation.29 | convolution fusion | flops 1074266112 | bytes 18088192 | tf_op jit(solution)/shard_map/dot_general | solution.py:72
  162.0 11.7 %psum.14 = f32[64]{0:T(128)S(1)} all-reduce(f32[64]{0:T(128)S(1)} %get-tuple-element.16), channel_id=1, replica_groups=mesh['batch'=8,'mp'=4] {'mp'}, use_global_device_ids=true, to_apply=%region_4.6 | all-reduce | flops 64 | bytes 512 | tf_op jit(solution)/shard_map/psum | solution.py:79
  173.7 0.8 multiply_convert_fusion
  174.6 0.0 all-gather.7.cloned.1.call-update
  174.6 0.2 all-reduce.2.cloned.1.call-start
  174.8 25.1 %all-gather.7.cloned.1.call-done = bf16[512,2048]{1,0:T(8,128)(2,1)} async-done(((bf16[64,2048]{1,0:T(8,128)(2,1)}), bf16[512,2048]{1,0:T(8,128)(2,1)}) %all-gather.7.cloned.1.call-update) | async-done | bytes 2097168 | tf_op jit(solution)/shard_map/all_gather | solution.py:82
  199.9 7.8 %convolution_convert_fusion.1 = bf16[512,1792]{1,0:T(8,128)(2,1)S(1)} fusion(bf16[512,2048]{1,0:T(8,128)(2,1)} %all-gather.7.cloned.1.call-done, bf16[2048,1792]{1,0:T(8,128)(2,1)} %param.22), kind=kOutput, calls=%fused_computation.8 | convolution fusion | flops 3759013888 | bytes 11272192 | tf_op jit(solution)/shard_map/dot_general | solution.py:84
  207.7 7.0 %convolution_convert_fusion.2 = bf16[512,1792]{1,0:T(8,128)(2,1)S(1)} fusion(bf16[512,2048]{1,0:T(8,128)(2,1)S(1)} %copy-done.5, bf16[2048,1792]{1,0:T(8,128)(2,1)} %param.21), kind=kOutput, calls=%fused_computation.9 | convolution fusion | flops 3759013888 | bytes 11272192 | tf_op jit(solution)/shard_map/dot_general | solution.py:83
  214.7 2.1 pad_maximum_fusion
  216.8 0.0 all-reduce.2.cloned.1.call-update
  216.9 0.0 reduce-scatter.2.cloned.1.call-start
  216.9 138.2 %all-reduce.2.cloned.1.call-done = bf16[512,3584]{1,0:T(8,128)(2,1)} async-done(((bf16[512,3584]{1,0:T(8,128)(2,1)}), bf16[512,3584]{1,0:T(8,128)(2,1)}) %all-reduce.2.cloned.1.call-update) | async-done | bytes 3670032 | tf_op jit(solution)/shard_map/psum | solution.py:87
  355.1 3.0 convert_element_type.62
  358.1 0.0 copy-start.1
  358.1 8.5 %convolution_convert_fusion = bf16[512,2048]{1,0:T(8,128)(2,1)} fusion(bf16[1792,2048]{1,0:T(8,128)(2,1)} %param.23, f32[512,3584]{1,0:T(8,128)S(1)} %convert_element_type.62), kind=kOutput, calls=%fused_computation.7 | convolution fusion | flops 3764649984 | bytes 16777216 | tf_op jit(solution)/shard_map/dot_general | solution.py:91
  366.6 0.0 reduce-scatter.2.cloned.1.call-update
  366.7 40.4 %reduce-scatter.2.cloned.1.call-done = bf16[64,2048]{1,0:T(8,128)(2,1)} async-done(((bf16[512,2048]{1,0:T(8,128)(2,1)}), bf16[64,2048]{1,0:T(8,128)(2,1)}) %reduce-scatter.2.cloned.1.call-update) | async-done | bytes 262160 | tf_op jit(solution)/shard_map/reduce_scatter | solution.py:90
  (17 shorter events, 0.1 us)
Async XLA Ops:
  7.2 1.5 copy-start
  7.2 54.1 %all-gather.9.cloned.1.call-start = ((), (), s32[]{:S(2)}) async-start(), calls=%async_computation.5 | async-start | bytes 2359296 | tf_op jit(solution)/shard_map/all_gather | solution.py:60
  11.9 20.4 %copy-start.6 = (s32[8]{0:T(128)S(1)}, s32[8]{0:T(128)}, u32[]{:S(2)}) copy-start(s32[8]{0:T(128)} %param.17) | copy-start | bytes 100
  12.0 21.6 %copy-start.4 = (s32[8]{0:T(128)S(1)}, s32[8]{0:T(128)}, u32[]{:S(2)}) copy-start(s32[8]{0:T(128)} %param.18) | copy-start | bytes 100
  29.7 123.4 %copy-start.2 = (bf16[1,64,2048]{2,1,0:T(8,128)(2,1)S(1)}, bf16[1,64,2048]{2,1,0:T(8,128)(2,1)}, u32[]{:S(2)}) copy-start(bf16[1,64,2048]{2,1,0:T(8,128)(2,1)} %param.13) | copy-start | bytes 786436
  31.5 121.6 %all-gather.5.cloned.1.call-start = ((), (), s32[]{:S(2)}) async-start(), calls=%async_computation.1 | async-start | bytes 18874368 | tf_op jit(solution)/shard_map/all_gather | solution.py:74
  32.3 167.6 %all-gather.7.cloned.1.call-start = ((), (), s32[]{:S(2)}) async-start(), calls=%async_computation.2 | async-start | bytes 2359296 | tf_op jit(solution)/shard_map/all_gather | solution.py:82
  153.1 20.6 %copy-start.3 = (f32[2048]{0:T(1024)S(1)}, f32[2048]{0:T(1024)}, u32[]{:S(2)}) copy-start(f32[2048]{0:T(1024)} %param.20) | copy-start | bytes 24580
  174.6 180.5 %all-reduce.2.cloned.1.call-start = ((), (), s32[]{:S(2)}) async-start(), calls=%async_computation.3 | async-start | bytes 7340032 | tf_op jit(solution)/shard_map/psum | solution.py:87
  199.9 7.8 %copy-start.5 = (bf16[512,2048]{1,0:T(8,128)(2,1)S(1)}, bf16[512,2048]{1,0:T(8,128)(2,1)}, u32[]{:S(2)}) copy-start(bf16[512,2048]{1,0:T(8,128)(2,1)} %all-gather.7.cloned.1.call-done) | copy-start | bytes 6291460
  216.9 190.2 %reduce-scatter.2.cloned.1.call-start = ((), (), s32[]{:S(2)}) async-start(), calls=%async_computation.4 | async-start | bytes 2359296 | tf_op jit(solution)/shard_map/reduce_scatter | solution.py:90
  358.1 49.0 %copy-start.1 = (bf16[1,64,512]{2,1,0:T(8,128)(2,1)S(1)}, bf16[1,64,512]{2,1,0:T(8,128)(2,1)}, u32[]{:S(2)}) copy-start(bf16[1,64,512]{2,1,0:T(8,128)(2,1)} %param.15) | copy-start | bytes 196612
Sparse Core Ops, SparseCore 0:
  31.6 29.6 all-gather.8
  63.2 89.8 all-gather.4
  174.7 25.1 all-gather.6
  217.0 138.0 all-reduce.1
  366.8 40.2 reduce-scatter.1
where the time goes:
time: 414 us
  waiting for transfers between devices  321 us (78%)
  matrix products  36.1 us (9%)
  blocking collectives  29.1 us (7%)
  between operations  14.6 us (4%)
  other arithmetic  7.56 us (2%)
  local copies, waits for them, and re-layouts  5.31 us (1%)
    psum x1, waiting for transfers between devices, body(): lax.psum(partial_value.astype(jnp.bfloat16), 'mp').astype(jnp.float32)  138 us
    all_gather x1, waiting for transfers between devices, body(): lax.all_gather(out_weight, 'batch', axis=0, tiled=True)  88.5 us
    reduce_scatter x1, waiting for transfers between devices, body(): lax.psum_scatter(jnp.dot(block_rows, down_weight, preferred_element_type=...  40.4 us
    all_gather x1, waiting for transfers between devices, body(): block_rows = lax.all_gather(picked_cols, 'batch', axis=0, tiled=True)  27.7 us
    all_gather x1, waiting for transfers between devices, body(): block_rows = lax.all_gather(normed, 'batch', axis=0, tiled=True)  25.1 us
    all_gather x1, blocking collectives, body(): all_heads = lax.all_gather(head_block, 'mp', axis=2, tiled=True)  17.4 us
    psum x1, blocking collectives, body(): squares = lax.psum(jnp.sum(hidden_state * hidden_state, axis=1), 'mp')  11.7 us
    dot_general x1, matrix products, body(): jnp.dot(mixed_heads, lax.all_gather(out_weight, 'batch', axis=0, tiled=Tr...  8.92 us
  transfers between devices with their start and end apart: 5, of which 5 were waited for; matrix products, arithmetic and copies ran while one was open for 1% of the time, Pallas kernels for 0%

commit v1 on v0

--- a/solution.py
+++ b/solution.py
@@ -9,6 +9,22 @@
 KV = 4
 HD = 128
 ABLATED = 8
+
+
+def gather_around(x, axis, dim):
+    ways, here, step = (lax.axis_size(axis), lax.axis_index(axis), x.shape[dim])
+    shape = [n * ways if d == dim else n for d, n in enumerate(x.shape)]
+    full = lax.dynamic_update_slice_in_dim(jnp.zeros(shape, x.dtype), x, here * step, axis=dim)
+    going_up = going_down = x
+    for far in range(1, ways // 2 + 1):
+        going_up = lax.ppermute(going_up, axis, [(d, (d + 1) % ways) for d in range(ways)])
+        full = lax.dynamic_update_slice_in_dim(full, going_up, (here - far) % ways * step, axis=dim)
+        if 2 * far < ways:
+            going_down = lax.ppermute(going_down, axis, [(d, (d - 1) % ways) for d in range(ways)])
+            full = lax.dynamic_update_slice_in_dim(
+                full, going_down, (here + far) % ways * step, axis=dim
+            )
+    return full
 
 
 def local_heads(query_states, key_states, value_states):
@@ -57,7 +73,7 @@
     picked_cols = jnp.take(stacked, ablated_heads, axis=2).reshape(
         prompts_here, length * ABLATED * HD
     )
-    block_rows = lax.all_gather(picked_cols, "batch", axis=0, tiled=True)
+    block_rows = gather_around(picked_cols, "batch", 0)
     selector = (sources[:, None] == jnp.arange(block_rows.shape[0])[None, :]).astype(jnp.bfloat16)
     picked = jnp.dot(selector, block_rows, preferred_element_type=jnp.float32)
     picked_four = picked.astype(jnp.bfloat16).reshape(prompts_here, length, ABLATED, HD)

time: 414 us -> 378 us (0.913)
  waiting for transfers between devices: 321 us -> 242 us
  local copies, waits for them, and re-layouts: 5.31 us -> 42.9 us
  starting transfers between devices: 0.38 us -> 8.39 us
    all_gather x1, waiting for transfers between devices: 88.5 us -> 6.25 us  [body(): lax.all_gather(out_weight, 'batch', axis=0, tiled=True)]
    dynamic_update_slice x0 -> x8, local copies, waits for them, and re-layouts: none -> 38.2 us  [the longest x4 19.1 us: gather_around(): lax.dynamic_update_slice_in_dim(full, going_up, (here - far) % ways * ste...]
    ppermute x0 -> x7, waiting for transfers between devices: none -> 31.6 us  [the longest x4 31.6 us: gather_around(): lax.ppermute(going_up, axis, [(d, (d + 1) % ways) for d in range(ways)])]
    all_gather x1 -> x0, waiting for transfers between devices: 27.7 us -> none  [body(): block_rows = lax.all_gather(picked_cols, 'batch', axis=0, tiled=True)]
    ppermute x0 -> x7, starting transfers between devices: none -> 8.05 us  [the longest x3 7.98 us: gather_around(): lax.ppermute(going_down, axis, [(d, (d - 1) % ways) for d in range(ways)])]
  transfers between devices with their start and end apart: 5 -> 11, of which waited for: 5 -> 7; matrix products, arithmetic and copies ran while one was open for 1% -> 12% of each run, Pallas kernels for 0% -> 0%
where the time goes in v1:
time: 378 us; the launch traced here: 377 us
  waiting for transfers between devices  242 us (64%)
  local copies, waits for them, and re-layouts  42.9 us (11%)
  matrix products  33.8 us (9%)
  blocking collectives  29.1 us (8%)
  between operations  14.8 us (4%)
  starting transfers between devices  8.39 us (2%)
  other arithmetic  6.27 us (2%)
    psum x1, waiting for transfers between devices, body(): lax.psum(partial_value.astype(jnp.bfloat16), 'mp').astype(jnp.float32)  138 us
    reduce_scatter x1, waiting for transfers between devices, body(): lax.psum_scatter(jnp.dot(block_rows, down_weight, preferred_element_type=...  40.4 us
    ppermute x4, waiting for transfers between devices, gather_around(): lax.ppermute(going_up, axis, [(d, (d + 1) % ways) for d in range(ways)])  31.6 us
    all_gather x1, waiting for transfers between devices, body(): block_rows = lax.all_gather(normed, 'batch', axis=0, tiled=True)  24.7 us
    dynamic_update_slice x4, local copies, waits for them, and re-layouts, gather_around(): lax.dynamic_update_slice_in_dim(full, going_up, (here - far) % ways * ste...  19.1 us
    all_gather x1, blocking collectives, body(): all_heads = lax.all_gather(head_block, 'mp', axis=2, tiled=True)  17.4 us
    dynamic_update_slice x3, local copies, waits for them, and re-layouts, gather_around(): lax.dynamic_update_slice_in_dim(full, going_down, (here + far) % ways * s...  14.7 us
    psum x1, blocking collectives, body(): squares = lax.psum(jnp.sum(hidden_state * hidden_state, axis=1), 'mp')  11.7 us
  transfers between devices with their start and end apart: 11, of which 7 were waited for; matrix products, arithmetic and copies ran while one was open for 12% of the time, Pallas kernels for 0%

profile of v1, /device:TPU:0, one launch (start us, length us, event | category | flops | bytes accessed | tf_op | source)
XLA Modules:
  0.0 377.1 jit_solution(8511479614229471169)
XLA Ops:
  7.2 0.7 all-gather.3.cloned.1.call-update
  8.0 0.9 copy.29
  9.0 0.6 gather_fusion.2
  9.6 0.9 bitcast_bitcast_fusion.1
  10.4 0.6 gather_fusion.1
  11.0 0.3 fusion.7
  11.3 0.1 fusion.39
  11.4 0.3 fusion.9
  11.7 17.4 %all_gather.9 = bf16[1,64,4096]{2,1,0:T(8,128)(2,1)S(1)} all-gather(bf16[1,64,1024]{2,1,0:T(8,128)(2,1)S(1)} %bitcast.107), channel_id=1, replica_groups=mesh['batch'=8,'mp'=4] {'mp'}, dimensions={2}, use_global_device_ids=true | all-gather | bytes 655360 | tf_op jit(solution)/shard_map/all_gather | solution.py:69
  29.0 0.1 copy.30
  29.1 0.2 copy.23
  29.4 0.6 gather_fusion
  30.0 0.1 select_bitcast_fusion
  30.1 0.1 copy.24
  30.2 0.1 reshape.199
  30.2 0.1 collective-permute-start
  30.3 2.6 collective-permute-start.1
  32.9 11.8 %collective-permute-done = bf16[1,65536]{1,0:T(2,128)(2,1)S(1)} collective-permute-done((bf16[1,65536]{1,0:T(2,128)(2,1)S(1)}, bf16[1,65536]{1,0:T(2,128)(2,1)S(1)}, u32[]{:S(2)}, u32[]{:S(2)}) %collective-permute-start) | collective-permute-done | bytes 131104 | tf_op jit(solution)/shard_map/ppermute | solution.py:20
  44.8 2.7 collective-permute-start.3
  47.5 11.1 %collective-permute-done.2 = bf16[1,65536]{1,0:T(2,128)(2,1)S(1)} collective-permute-done((bf16[1,65536]{1,0:T(2,128)(2,1)S(1)}, bf16[1,65536]{1,0:T(2,128)(2,1)S(1)}, u32[]{:S(2)}, u32[]{:S(2)}) %collective-permute-start.2) | collective-permute-done | bytes 131104 | tf_op jit(solution)/shard_map/ppermute | solution.py:20
  58.5 2.6 collective-permute-start.5
  61.2 8.7 %collective-permute-done.4 = bf16[1,65536]{1,0:T(2,128)(2,1)S(1)} collective-permute-done((bf16[1,65536]{1,0:T(2,128)(2,1)S(1)}, bf16[1,65536]{1,0:T(2,128)(2,1)S(1)}, u32[]{:S(2)}, u32[]{:S(2)}) %collective-permute-start.4) | collective-permute-done | bytes 131104 | tf_op jit(solution)/shard_map/ppermute | solution.py:20
  69.9 0.1 broadcast_in_dim.61
  70.0 4.4 %dynamic_update_slice.24 = bf16[8,65536]{1,0:T(8,128)(2,1)S(1)} dynamic-update-slice(bf16[8,65536]{1,0:T(8,128)(2,1)S(1)} %broadcast_in_dim.61, bf16[1,65536]{1,0:T(2,128)(2,1)S(1)} %reshape.199, s32[]{:T(128)S(6)} %select_n.115, s32[]{:T(128)} %constant.114.clone.1) | dynamic-update-slice | bytes 262148 | tf_op jit(solution)/shard_map/dynamic_update_slice | solution.py:17
  74.5 0.6 dynamic-slice.2
  75.7 0.1 fusion.27
  75.8 4.4 %dynamic_update_slice.25 = bf16[8,65536]{1,0:T(8,128)(2,1)S(1)} dynamic-update-slice(bf16[8,65536]{1,0:T(8,128)(2,1)S(1)} %dynamic_update_slice.24, bf16[1,65536]{1,0:T(2,128)(2,1)S(1)} %collective-permute-done, s32[]{:T(128)S(6)} %select_n.117, s32[]{:T(128)} %constant.114.clone.1) | dynamic-update-slice | bytes 262148 | tf_op jit(solution)/shard_map/dynamic_update_slice | solution.py:21
  80.2 4.4 %dynamic_update_slice.26 = bf16[8,65536]{1,0:T(8,128)(2,1)S(1)} dynamic-update-slice(bf16[8,65536]{1,0:T(8,128)(2,1)S(1)} %dynamic_update_slice.25, bf16[1,65536]{1,0:T(2,128)(2,1)S(1)} %collective-permute-done.1, s32[]{:T(128)S(6)} %select_n.119, s32[]{:T(128)} %constant.114.clone.1) | dynamic-update-slice | bytes 262148 | tf_op jit(solution)/shard_map/dynamic_update_slice | solution.py:24
  84.7 4.4 %dynamic_update_slice.27 = bf16[8,65536]{1,0:T(8,128)(2,1)S(1)} dynamic-update-slice(bf16[8,65536]{1,0:T(8,128)(2,1)S(1)} %dynamic_update_slice.26, bf16[1,65536]{1,0:T(2,128)(2,1)S(1)} %collective-permute-done.2, s32[]{:T(128)S(6)} %select_n.121, s32[]{:T(128)} %constant.114.clone.1) | dynamic-update-slice | bytes 262148 | tf_op jit(solution)/shard_map/dynamic_update_slice | solution.py:21
  89.1 4.4 %dynamic_update_slice.28 = bf16[8,65536]{1,0:T(8,128)(2,1)S(1)} dynamic-update-slice(bf16[8,65536]{1,0:T(8,128)(2,1)S(1)} %dynamic_update_slice.27, bf16[1,65536]{1,0:T(2,128)(2,1)S(1)} %collective-permute-done.3, s32[]{:T(128)S(6)} %select_n.123, s32[]{:T(128)} %constant.114.clone.1) | dynamic-update-slice | bytes 262148 | tf_op jit(solution)/shard_map/dynamic_update_slice | solution.py:24
  93.6 4.4 %dynamic_update_slice.29 = bf16[8,65536]{1,0:T(8,128)(2,1)S(1)} dynamic-update-slice(bf16[8,65536]{1,0:T(8,128)(2,1)S(1)} %dynamic_update_slice.28, bf16[1,65536]{1,0:T(2,128)(2,1)S(1)} %collective-permute-done.4, s32[]{:T(128)S(6)} %select_n.125, s32[]{:T(128)} %constant.114.clone.1) | dynamic-update-slice | bytes 262148 | tf_op jit(solution)/shard_map/dynamic_update_slice | solution.py:21
  98.0 5.8 %dynamic_update_slice.30 = bf16[8,65536]{1,0:T(8,128)(2,1)S(1)} dynamic-update-slice(bf16[8,65536]{1,0:T(8,128)(2,1)S(1)} %dynamic_update_slice.29, bf16[1,65536]{1,0:T(2,128)(2,1)} %collective-permute-done.5, s32[]{:T(128)S(6)} %select_n.127, s32[]{:T(128)} %constant.114.clone.1) | dynamic-update-slice | bytes 262148 | tf_op jit(solution)/shard_map/dynamic_update_slice | solution.py:24
  103.9 5.8 %dynamic_update_slice.31 = bf16[8,65536]{1,0:T(8,128)(2,1)S(1)} dynamic-update-slice(bf16[8,65536]{1,0:T(8,128)(2,1)S(1)} %dynamic_update_slice.30, bf16[1,65536]{1,0:T(2,128)(2,1)} %collective-permute-done.6, s32[]{:T(128)S(6)} %select_n.129, s32[]{:T(128)} %constant.114.clone.1) | dynamic-update-slice | bytes 262148 | tf_op jit(solution)/shard_map/dynamic_update_slice | solution.py:21
  109.7 0.4 fusion.30
  110.1 0.4 fusion.10
  110.5 6.2 %all-gather.3.cloned.1.call-done = bf16[4096,2048]{1,0:T(8,128)(2,1)} async-done(((bf16[512,2048]{1,0:T(8,128)(2,1)}), bf16[4096,2048]{1,0:T(8,128)(2,1)}) %all-gather.3.cloned.1.call-update) | async-done | bytes 16777232 | tf_op jit(solution)/shard_map/all_gather | solution.py:90
  116.8 9.0 %multiply_reduce_fusion = (f32[64]{0:T(128)S(1)}, f32[64,2048]{1,0:T(8,128)S(1)}) fusion(bf16[1,64,2048]{2,1,0:T(8,128)(2,1)S(1)} %copy-done.2, bf16[4096,2048]{1,0:T(8,128)(2,1)} %all-gather.3.cloned.1.call-done, bf16[8,8,32,128]{3,2,1,0:T(8,128)(2,1)S(1)} %bitcast.104), kind=kOutput, calls=%fused_computation.26 | convolution fusion | flops 1074266112 | bytes 18088192 | tf_op jit(solution)/shard_map/dot_general | solution.py:88
  125.8 11.7 %psum.14 = f32[64]{0:T(128)S(1)} all-reduce(f32[64]{0:T(128)S(1)} %get-tuple-element.16), channel_id=1, replica_groups=mesh['batch'=8,'mp'=4] {'mp'}, use_global_device_ids=true, to_apply=%region_4.6 | all-reduce | flops 64 | bytes 512 | tf_op jit(solution)/shard_map/psum | solution.py:95
  137.5 0.8 multiply_convert_fusion
  138.3 0.2 all-reduce.2.cloned.1.call-start
  138.6 24.7 %all-gather.5.cloned.1.call-done = bf16[512,2048]{1,0:T(8,128)(2,1)} async-done(((bf16[64,2048]{1,0:T(8,128)(2,1)}), bf16[512,2048]{1,0:T(8,128)(2,1)}) %all-gather.5.cloned.1.call-update) | async-done | bytes 2097168 | tf_op jit(solution)/shard_map/all_gather | solution.py:98
  163.3 7.8 %convolution_convert_fusion.1 = bf16[512,1792]{1,0:T(8,128)(2,1)S(1)} fusion(bf16[512,2048]{1,0:T(8,128)(2,1)} %all-gather.5.cloned.1.call-done, bf16[2048,1792]{1,0:T(8,128)(2,1)} %param.22), kind=kOutput, calls=%fused_computation.8 | convolution fusion | flops 3759013888 | bytes 11272192 | tf_op jit(solution)/shard_map/dot_general | solution.py:100
  171.1 7.0 %convolution_convert_fusion.2 = bf16[512,1792]{1,0:T(8,128)(2,1)S(1)} fusion(bf16[512,2048]{1,0:T(8,128)(2,1)S(1)} %copy-done.5, bf16[2048,1792]{1,0:T(8,128)(2,1)} %param.21), kind=kOutput, calls=%fused_computation.9 | convolution fusion | flops 3759013888 | bytes 11272192 | tf_op jit(solution)/shard_map/dot_general | solution.py:99
  178.2 2.1 pad_maximum_fusion
  180.4 138.2 %all-reduce.2.cloned.1.call-done = bf16[512,3584]{1,0:T(8,128)(2,1)} async-done(((bf16[512,3584]{1,0:T(8,128)(2,1)}), bf16[512,3584]{1,0:T(8,128)(2,1)}) %all-reduce.2.cloned.1.call-update) | async-done | bytes 3670032 | tf_op jit(solution)/shard_map/psum | solution.py:103
  318.5 3.0 convert_element_type.62
  321.5 8.7 %convolution_convert_fusion = bf16[512,2048]{1,0:T(8,128)(2,1)} fusion(bf16[1792,2048]{1,0:T(8,128)(2,1)} %param.23, f32[512,3584]{1,0:T(8,128)S(1)} %convert_element_type.62), kind=kOutput, calls=%fused_computation.7 | convolution fusion | flops 3764649984 | bytes 16777216 | tf_op jit(solution)/shard_map/dot_general | solution.py:107
  330.2 40.4 %reduce-scatter.2.cloned.1.call-done = bf16[64,2048]{1,0:T(8,128)(2,1)} async-done(((bf16[512,2048]{1,0:T(8,128)(2,1)}), bf16[64,2048]{1,0:T(8,128)(2,1)}) %reduce-scatter.2.cloned.1.call-update) | async-done | bytes 262160 | tf_op jit(solution)/shard_map/reduce_scatter | solution.py:106
  (37 shorter events, 0.3 us)
Async XLA Ops:
  7.2 1.8 copy-start
  7.2 109.6 %all-gather.3.cloned.1.call-start = ((), (), s32[]{:S(2)}) async-start(), calls=%async_computation.1 | async-start | bytes 18874368 | tf_op jit(solution)/shard_map/all_gather | solution.py:90
  7.9 21.4 %copy-start.4 = (s32[8]{0:T(128)S(1)}, s32[8]{0:T(128)}, u32[]{:S(2)}) copy-start(s32[8]{0:T(128)} %param.18) | copy-start | bytes 100
  7.9 155.4 %all-gather.5.cloned.1.call-start = ((), (), s32[]{:S(2)}) async-start(), calls=%async_computation.2 | async-start | bytes 2359296 | tf_op jit(solution)/shard_map/all_gather | solution.py:98
  11.4 63.1 %copy-start.6 = (s32[8]{0:T(128)S(1)}, s32[8]{0:T(128)}, u32[]{:S(2)}) copy-start(s32[8]{0:T(128)} %param.17) | copy-start | bytes 100
  30.2 14.5 %collective-permute-start = (bf16[1,65536]{1,0:T(2,128)(2,1)S(1)}, bf16[1,65536]{1,0:T(2,128)(2,1)S(1)}, u32[]{:S(2)}, u32[]{:S(2)}) collective-permute-start(bf16[1,65536]{1,0:T(2,128)(2,1)S(1)} %reshape.199), channel_id=1, source_target_pairs={{0,4},{4,8},{8,12},{12,16},{16,20},{20,24},{24,28},{28,0},{1,5},{5... | collective-permute-start | bytes 393224 | tf_op jit(solution)/shard_map/ppermute | solution.py:20
  30.3 14.5 %collective-permute-start.1 = (bf16[1,65536]{1,0:T(2,128)(2,1)S(1)}, bf16[1,65536]{1,0:T(2,128)(2,1)S(1)}, u32[]{:S(2)}, u32[]{:S(2)}) collective-permute-start(bf16[1,65536]{1,0:T(2,128)(2,1)S(1)} %reshape.199), channel_id=1, source_target_pairs={{0,28},{4,0},{8,4},{12,8},{16,12},{20,16},{24,20},{28,24},{1,29},{... | collective-permute-start | bytes 393224 | tf_op jit(solution)/shard_map/ppermute | solution.py:23
  44.8 13.8 %collective-permute-start.2 = (bf16[1,65536]{1,0:T(2,128)(2,1)S(1)}, bf16[1,65536]{1,0:T(2,128)(2,1)S(1)}, u32[]{:S(2)}, u32[]{:S(2)}) collective-permute-start(bf16[1,65536]{1,0:T(2,128)(2,1)S(1)} %collective-permute-done), channel_id=1, source_target_pairs={{0,4},{4,8},{8,12},{12,16},{16,20},{20,24},{24,28},{28,0},{1,5},{5... | collective-permute-start | bytes 393224 | tf_op jit(solution)/shard_map/ppermute | solution.py:20
  44.8 13.8 %collective-permute-start.3 = (bf16[1,65536]{1,0:T(2,128)(2,1)S(1)}, bf16[1,65536]{1,0:T(2,128)(2,1)S(1)}, u32[]{:S(2)}, u32[]{:S(2)}) collective-permute-start(bf16[1,65536]{1,0:T(2,128)(2,1)S(1)} %collective-permute-done.1), channel_id=1, source_target_pairs={{0,28},{4,0},{8,4},{12,8},{16,12},{20,16},{24,20},{28,24},{1,29},{... | collective-permute-start | bytes 393224 | tf_op jit(solution)/shard_map/ppermute | solution.py:23
  58.5 11.4 %collective-permute-start.4 = (bf16[1,65536]{1,0:T(2,128)(2,1)S(1)}, bf16[1,65536]{1,0:T(2,128)(2,1)S(1)}, u32[]{:S(2)}, u32[]{:S(2)}) collective-permute-start(bf16[1,65536]{1,0:T(2,128)(2,1)S(1)} %collective-permute-done.2), channel_id=1, source_target_pairs={{0,4},{4,8},{8,12},{12,16},{16,20},{20,24},{24,28},{28,0},{1,5},{5... | collective-permute-start | bytes 393224 | tf_op jit(solution)/shard_map/ppermute | solution.py:20
  58.5 39.5 %collective-permute-start.5 = (bf16[1,65536]{1,0:T(2,128)(2,1)S(1)}, bf16[1,65536]{1,0:T(2,128)(2,1)}, u32[]{:S(2)}, u32[]{:S(2)}) collective-permute-start(bf16[1,65536]{1,0:T(2,128)(2,1)S(1)} %collective-permute-done.3), channel_id=1, source_target_pairs={{0,28},{4,0},{8,4},{12,8},{16,12},{20,16},{24,20},{28,24},{1,29},{... | collective-permute-start | bytes 393224 | tf_op jit(solution)/shard_map/ppermute | solution.py:23
  69.9 33.9 %collective-permute-start.6 = (bf16[1,65536]{1,0:T(2,128)(2,1)S(1)}, bf16[1,65536]{1,0:T(2,128)(2,1)}, u32[]{:S(2)}, u32[]{:S(2)}) collective-permute-start(bf16[1,65536]{1,0:T(2,128)(2,1)S(1)} %collective-permute-done.4), channel_id=1, source_target_pairs={{0,4},{4,8},{8,12},{12,16},{16,20},{20,24},{24,28},{28,0},{1,5},{5... | collective-permute-start | bytes 393224 | tf_op jit(solution)/shard_map/ppermute | solution.py:20
  70.0 46.8 %copy-start.2 = (bf16[1,64,2048]{2,1,0:T(8,128)(2,1)S(1)}, bf16[1,64,2048]{2,1,0:T(8,128)(2,1)}, u32[]{:S(2)}) copy-start(bf16[1,64,2048]{2,1,0:T(8,128)(2,1)} %param.13) | copy-start | bytes 786436
  116.8 20.7 %copy-start.3 = (f32[2048]{0:T(1024)S(1)}, f32[2048]{0:T(1024)}, u32[]{:S(2)}) copy-start(f32[2048]{0:T(1024)} %param.20) | copy-start | bytes 24580
  138.3 180.2 %all-reduce.2.cloned.1.call-start = ((), (), s32[]{:S(2)}) async-start(), calls=%async_computation.3 | async-start | bytes 7340032 | tf_op jit(solution)/shard_map/psum | solution.py:103
  163.3 7.8 %copy-start.5 = (bf16[512,2048]{1,0:T(8,128)(2,1)S(1)}, bf16[512,2048]{1,0:T(8,128)(2,1)}, u32[]{:S(2)}) copy-start(bf16[512,2048]{1,0:T(8,128)(2,1)} %all-gather.5.cloned.1.call-done) | copy-start | bytes 6291460
  180.3 190.3 %reduce-scatter.2.cloned.1.call-start = ((), (), s32[]{:S(2)}) async-start(), calls=%async_computation.4 | async-start | bytes 2359296 | tf_op jit(solution)/shard_map/reduce_scatter | solution.py:106
  321.5 49.1 %copy-start.1 = (bf16[1,64,512]{2,1,0:T(8,128)(2,1)S(1)}, bf16[1,64,512]{2,1,0:T(8,128)(2,1)}, u32[]{:S(2)}) copy-start(bf16[1,64,512]{2,1,0:T(8,128)(2,1)} %param.15) | copy-start | bytes 196612
Sparse Core Ops, SparseCore 0:
  9.9 106.8 all-gather.2
  138.5 24.7 all-gather.4
  180.4 138.0 all-reduce.1
  330.3 40.2 reduce-scatter.1
